TPU v7x, 512 devices: a whole 4x8x8 slice. The times are simulated.
512 devices in a mesh: section: 2 (over core), seq: 32 (over x, z), head: 8 (over y).
Axes of the slice: x: 4, y: 8, z: 8, core: 2. Of those that a mesh axis runs over, the one named last changes fastest.
Arguments:
- prompt_states: bfloat16 [16384, 7168], P(('section', 'seq'), 'head'), may hold values from -6 to 6
- w_down: bfloat16 [7168, 576], P('head'), may hold values from -0.0625 to 0.0625
- kv_gain: float32 [512], replicated, may hold values from 0.1 to 1.9
- prompt_lengths: int32 [8], replicated, may hold values from 1 to 4096, 16384 in all
- block_owner: int32 [2048], replicated, may hold values from 0 to 31, as said below
- row_prompt: int32 [64], replicated, may hold values from 0 to 7
- queries: bfloat16 [2, 64, 128, 192], P(None, 'seq', ('section', 'head')), may hold values from -64 to 64
- new_kv: bfloat16 [2, 64, 576], P(None, 'seq'), may hold values from -64 to 64
- w_uk: bfloat16 [128, 128, 512], P(('section', 'head')), may hold values from -0.5 to 0.5
- w_uv: bfloat16 [128, 512, 128], P(('section', 'head')), may hold values from -0.25 to 0.25
Outputs:
- attended: bfloat16 [2, 64, 128, 128], P(None, 'seq', ('section', 'head'))
- decode_cache: bfloat16 [16384, 576], P('seq')
Inputs may be any that keep to these rules, and one draw needn't show every extreme that they name: `block_owner`: within each aligned group of 32 blocks, the blocks of one prompt device, every seq index appears exactly 1 times.
All inputs are finite; a program needn't handle non-finite values.
Results may differ from a plain program's by a relative error of at most 0.0075.
Values may be sent and summed in bfloat16 or wider, within the bound.
A program may use at most 64 MiB of HBM per device.

v0:
```python
import math

import jax
import jax.numpy as jnp
from jax import lax
from jax.sharding import PartitionSpec as P

BLOCK = 8


def prompt_table(prompt_lengths, token_ids):
    ends = jnp.cumsum(prompt_lengths)
    starts = ends - prompt_lengths
    segment = jnp.sum((token_ids[..., None] >= ends).astype(jnp.int32), axis=-1)
    chosen = (segment[..., None] == jnp.arange(prompt_lengths.shape[0], dtype=jnp.int32)).astype(
        jnp.int32
    )
    position = token_ids - jnp.sum(chosen * starts, axis=-1)
    return (segment, position)


def finish_rows(projected, kv_gain, position):
    latent_width = kv_gain.shape[0]
    latent = projected[..., :latent_width]
    rotary = projected[..., latent_width:]
    inverse = lax.rsqrt(jnp.mean(latent * latent, axis=-1, keepdims=True) + 1e-06)
    normed = latent * inverse * kv_gain
    half_width = rotary.shape[-1] // 2
    frequency = 10000.0 ** (-2.0 * jnp.arange(half_width, dtype=jnp.float32) / rotary.shape[-1])
    angle = position[..., None].astype(jnp.float32) * frequency
    cosine = jnp.cos(angle)
    sine = jnp.sin(angle)
    first_half = rotary[..., :half_width]
    second_half = rotary[..., half_width:]
    turned = jnp.concatenate(
        [first_half * cosine - second_half * sine, second_half * cosine + first_half * sine],
        axis=-1,
    )
    return jnp.concatenate([normed, turned], axis=-1)


def on_device(
    prompt_states,
    w_down,
    kv_gain,
    prompt_lengths,
    block_owner,
    row_prompt,
    queries,
    new_kv,
    w_uk,
    w_uv,
):
    section_count = lax.axis_size("section")
    seq_count = lax.axis_size("seq")
    seq_index = lax.axis_index("seq")
    pre_tokens = prompt_states.shape[0]
    blocks_here = pre_tokens // BLOCK
    per_peer = blocks_here // seq_count
    latent_width = kv_gain.shape[0]
    total_width = w_down.shape[1]
    sender = lax.axis_index("section") * seq_count + seq_index
    projected = jnp.dot(prompt_states, w_down, preferred_element_type=jnp.float32)
    projected = projected.reshape(blocks_here, BLOCK, total_width)
    token_ids = (sender * pre_tokens + jnp.arange(pre_tokens, dtype=jnp.int32)).reshape(
        blocks_here, BLOCK
    )
    local_owner = lax.dynamic_slice_in_dim(block_owner, sender * blocks_here, blocks_here, 0)
    send_order = jnp.argsort(local_owner, stable=True)
    summed = lax.psum(projected, "head")
    position = prompt_table(prompt_lengths, token_ids)[1]
    finished = finish_rows(summed, kv_gain, position).astype(jnp.bfloat16)
    packed = finished[send_order].reshape(seq_count, per_peer, 1, BLOCK, total_width)
    arrived = lax.all_to_all(packed, "seq", split_axis=0, concat_axis=0, tiled=True)
    cache_blocks = lax.all_gather(arrived, "section", axis=2, tiled=True)
    cache_count = seq_count * per_peer * section_count * BLOCK
    cache_keys = cache_blocks.reshape(cache_count, total_width)
    owner_table = block_owner.reshape(section_count * seq_count, blocks_here)
    sorted_blocks = jnp.argsort(owner_table, axis=1, stable=True)
    sorted_blocks = sorted_blocks.reshape(section_count * seq_count, seq_count, per_peer)
    own_blocks = lax.dynamic_index_in_dim(sorted_blocks, seq_index, axis=1, keepdims=False)
    block_ids = (
        jnp.arange(section_count * seq_count, dtype=jnp.int32)[:, None] * blocks_here + own_blocks
    )
    block_ids = block_ids.reshape(section_count, seq_count, per_peer).transpose(1, 2, 0)
    cache_ids = (block_ids[..., None] * BLOCK + jnp.arange(BLOCK, dtype=jnp.int32)).reshape(
        cache_count
    )
    cache_segment = prompt_table(prompt_lengths, cache_ids)[0]
    nope_width = w_uk.shape[1]
    score_scale = 1.0 / math.sqrt(queries.shape[-1])
    piece = lax.all_gather(queries, "seq", axis=1, tiled=True)
    absorbed = jnp.einsum(
        "srhn,hnl->srhl", piece[..., :nope_width], w_uk, preferred_element_type=jnp.float32
    )
    full_query = jnp.concatenate([absorbed.astype(jnp.bfloat16), piece[..., nope_width:]], axis=-1)
    own_rows = queries.shape[1]
    row_start = seq_index * own_rows
    step_count = queries.shape[0]
    scores = (
        jnp.einsum("srhk,tk->srht", full_query, cache_keys, preferred_element_type=jnp.float32)
        * score_scale
    )
    allowed = cache_segment[None, :] == row_prompt[:, None]
    scores = jnp.where(allowed[None, :, None, :], scores, -jnp.inf)
    own_query = lax.dynamic_slice_in_dim(full_query, row_start, own_rows, 1)
    own_scores = (
        jnp.einsum("srhk,urk->srhu", own_query, new_kv, preferred_element_type=jnp.float32)
        * score_scale
    )
    causal = jnp.arange(step_count)[:, None] >= jnp.arange(step_count)[None, :]
    own_scores = jnp.where(causal[:, None, None, :], own_scores, -jnp.inf)
    local_top = jnp.max(scores, axis=-1)
    own_slice = lax.dynamic_slice_in_dim(local_top, row_start, own_rows, 1)
    local_top = lax.dynamic_update_slice_in_dim(
        local_top, jnp.maximum(own_slice, jnp.max(own_scores, axis=-1)), row_start, 1
    )
    row_top = lax.pmax(local_top, "seq")
    weights = jnp.exp(scores - row_top[..., None])
    denominator = jnp.sum(weights, axis=-1)
    weighted = jnp.einsum(
        "srht,tl->srhl",
        weights.astype(jnp.bfloat16),
        cache_keys[:, :latent_width],
        preferred_element_type=jnp.float32,
    )
    own_top = lax.dynamic_slice_in_dim(row_top, row_start, own_rows, 1)
    own_weights = jnp.exp(own_scores - own_top[..., None])
    own_denominator = jnp.sum(own_weights, axis=-1)
    own_weighted = jnp.einsum(
        "srhu,url->srhl",
        own_weights.astype(jnp.bfloat16),
        new_kv[..., :latent_width],
        preferred_element_type=jnp.float32,
    )
    up_float = w_uv.astype(jnp.float32)
    weighted_share, denominator_share = (
        lax.psum_scatter(weighted, "seq", scatter_dimension=1, tiled=True),
        lax.psum_scatter(denominator, "seq", scatter_dimension=1, tiled=True),
    )
    context = (weighted_share + own_weighted) / (denominator_share + own_denominator)[..., None]
    attended = jnp.einsum("srhl,hlv->srhv", context, up_float, precision=lax.Precision.HIGHEST)
    return (attended.astype(jnp.bfloat16), cache_keys)


def solution(mesh):
    placed = (
        P(("section", "seq"), "head"),
        P("head", None),
        P(),
        P(),
        P(),
        P(),
        P(None, "seq", ("section", "head"), None),
        P(None, "seq", None),
        P(("section", "head"), None, None),
        P(("section", "head"), None, None),
    )
    return jax.shard_map(
        on_device,
        mesh=mesh,
        in_specs=placed,
        out_specs=(P(None, "seq", ("section", "head"), None), P("seq", None)),
        check_vma=False,
    )
```

profile of v0, /device:TPU:8, one launch (start us, length us, event | category | flops | bytes accessed | tf_op | source)
XLA Modules:
  0.0 492.6 jit_solution(14580200514850031337)
XLA Ops:
  7.2 0.0 copy-start
  7.2 0.0 copy-start.3
  7.2 0.0 copy-start.4
  7.2 0.0 copy-start.8
  7.2 0.0 all-reduce.3.cloned.1.call-start
  7.3 2.9 convolution_bitcast_fusion
  10.1 0.0 all-reduce.3.cloned.1.call-update
  10.2 0.0 copy-done.3
  10.2 55.7 %all_gather.6 = bf16[2,64,8,192]{3,2,0,1:T(8,128)(2,1)S(1)} all-gather(bf16[2,2,8,192]{3,2,0,1:T(8,128)(2,1)S(1)} %copy.77), channel_id=1, replica_groups=mesh['section'=2,'seq'=32,'head'=8] {'seq'}, dimensions={1}, use_global_device_ids=true | all-gather | bytes 405504 | tf_op jit(solution)/shard_map/all_gather | solution.py:92
  66.0 0.0 copy-done.4
  66.0 0.1 reshape.158
  66.0 0.1 dynamic_slice.14
  66.1 0.0 copy-done.8
  66.1 0.2 reduce-window.8
  66.3 1.6 sort.35
  67.9 0.1 convert_reduce_fusion
  68.0 0.1 select_reduce_fusion
  68.1 0.1 copy.81
  68.2 0.1 copy.75
  68.3 0.8 sort.34
  69.1 0.1 mul.118
  69.2 0.1 copy.76
  69.3 0.1 copy.110
  69.4 0.1 copy.109
  69.4 0.0 copy-done
  69.5 0.4 fusion.34
  69.9 0.1 convert_bitcast_fusion
  70.0 0.1 fusion.22
  70.1 0.0 copy-start.6
  70.1 1.2 pad_maximum_fusion
  71.3 0.1 iota_add_fusion
  71.4 22.8 %all-reduce.3.cloned.1.call-done = f32[32,8,576]{2,1,0:T(8,128)} async-done(((f32[32,8,576]{2,1,0:T(8,128)}), f32[32,8,576]{2,1,0:T(8,128)}) %all-reduce.3.cloned.1.call-update) | async-done | bytes 589840 | tf_op jit(solution)/shard_map/psum | solution.py:70
  94.3 1.2 multiply_reduce_fusion
  95.4 1.6 fusion.18
  97.0 0.0 copy-done.6
  97.0 1.2 multiply_convert_fusion
  98.2 0.0 copy-start.1
  98.2 0.1 pad_maximum_fusion.1
  98.3 1.3 gather_fusion
  99.6 10.2 %all-to-all-start = ((bf16[32,1,1,8,576]{4,3,2,1,0:T(8,128)(2,1)}), bf16[32,1,1,8,576]{4,3,2,1,0:T(8,128)(2,1)S(1)}, u32[]{:S(2)}, u32[]{:S(2)}) async-start(bf16[32,1,1,8,576]{4,3,2,1,0:T(8,128)(2,1)} %bitcast.10), calls=%async_computation | async-start | bytes 655360 | tf_op jit(solution)/shard_map/all_to_all | solution.py:74
  109.8 0.0 reduce-scatter.2.cloned.1.call-start
  109.9 0.1 add.101
  110.0 0.1 convert_reduce_fusion.1
  110.1 0.0 copy-done.7
  110.1 0.1 broadcast_compare_fusion
  110.2 0.0 copy-done.5
  110.2 0.2 fusion.33
  110.4 10.6 %all-to-all-done = bf16[32,1,1,8,576]{4,3,2,1,0:T(8,128)(2,1)S(1)} async-done(((bf16[32,1,1,8,576]{4,3,2,1,0:T(8,128)(2,1)}), bf16[32,1,1,8,576]{4,3,2,1,0:T(8,128)(2,1)S(1)}, u32[]{:S(2)}, u32[]{:S(2)}) %all-to-all-start) | async-done | bytes 294944 | tf_op jit(solution)/shard_map/all_to_all | solution.py:74
  121.0 2.3 all_gather.7
  123.2 0.1 copy.84
  123.3 0.0 copy-done.1
  123.3 2.5 fusion
  125.9 140.0 %pmax.7 = f32[2,64,8]{2,1,0:T(8,128)S(1)} all-reduce(f32[2,64,8]{2,1,0:T(8,128)S(1)} %fusion.28), channel_id=1, replica_groups=mesh['section'=2,'seq'=32,'head'=8] {'seq'}, use_global_device_ids=true, to_apply=%region_10.11 | all-reduce | flops 1024 | bytes 8192 | tf_op jit(solution)/shard_map/pmax | solution.py:118
  265.9 2.3 fusion.1
  268.2 2.1 fusion.11
  270.2 0.0 reduce-scatter.2.cloned.1.call-update
  270.3 1.3 dynamic-slice.4
  272.3 1.1 copy.97
  273.4 0.1 copy.94
  273.4 137.8 %all-reduce = f32[2,64,8]{2,0,1:T(2,128)S(1)} all-reduce(f32[2,64,8]{2,0,1:T(2,128)S(1)} %copy.94), channel_id=3, replica_groups=mesh['section'=2,'seq'=32,'head'=8] {'seq'}, use_global_device_ids=true, to_apply=%region_13.14.clone | all-reduce | flops 1024 | bytes 8192
  411.2 72.3 %reduce-scatter.2.cloned.1.call-done = f32[2,2,8,512]{3,2,0,1:T(8,128)} async-done(((f32[2,64,8,512]{3,2,0,1:T(8,128)}), f32[2,2,8,512]{3,2,0,1:T(8,128)}) %reduce-scatter.2.cloned.1.call-update) | async-done | bytes 65552 | tf_op jit(solution)/shard_map/reduce_scatter | solution.py:138
  483.5 1.0 fusion.6
  484.6 0.6 fusion.7
  485.2 0.6 copy.96
  (24 shorter events, 0.3 us)
Async XLA Ops:
  7.2 62.3 %copy-start = (bf16[8,128,512]{2,1,0:T(8,128)(2,1)S(1)}, bf16[8,128,512]{2,1,0:T(8,128)(2,1)}, u32[]{:S(2)}) copy-start(bf16[8,128,512]{2,1,0:T(8,128)(2,1)} %param.18) | copy-start | bytes 3145732
  7.2 3.0 copy-start.3
  7.2 58.8 %copy-start.4 = (s32[2048]{0:T(1024)S(1)}, s32[2048]{0:T(1024)}, u32[]{:S(2)}) copy-start(s32[2048]{0:T(1024)} %param.14) | copy-start | bytes 24580
  7.2 58.9 %copy-start.8 = (s32[8]{0:T(128)S(1)}, s32[8]{0:T(128)}, u32[]{:S(2)}) copy-start(s32[8]{0:T(128)} %param.13) | copy-start | bytes 100
  7.2 87.1 %all-reduce.3.cloned.1.call-start = ((), (), s32[]{:S(2)}) async-start(), calls=%async_computation.2 | async-start | bytes 1310720 | tf_op jit(solution)/shard_map/psum | solution.py:70
  70.1 26.9 %copy-start.6 = (f32[512]{0:T(512)S(1)}, f32[512]{0:T(512)}, u32[]{:S(2)}) copy-start(f32[512]{0:T(512)} %param.12) | copy-start | bytes 6148
  71.3 38.7 %copy-start.7 = (s32[64]{0:T(128)S(1)}, s32[64]{0:T(128)}, u32[]{:S(2)}) copy-start(s32[64]{0:T(128)} %param.15) | copy-start | bytes 772
  71.3 38.8 %copy-start.5 = (bf16[2,2,576]{2,1,0:T(2,128)(2,1)S(1)}, bf16[2,2,576]{2,1,0:T(2,128)(2,1)}, u32[]{:S(2)}) copy-start(bf16[2,2,576]{2,1,0:T(2,128)(2,1)} %param.17) | copy-start | bytes 13828
  98.2 25.1 %copy-start.1 = (bf16[2,64,8,576]{3,1,0,2:T(8,128)(2,1)S(1)}, bf16[2,64,8,576]{3,1,0,2:T(8,128)(2,1)}, u32[]{:S(2)}) copy-start(bf16[2,64,8,576]{3,1,0,2:T(8,128)(2,1)} %pad_maximum_fusion) | copy-start | bytes 3538948
  99.6 21.4 %all-to-all-start = ((bf16[32,1,1,8,576]{4,3,2,1,0:T(8,128)(2,1)}), bf16[32,1,1,8,576]{4,3,2,1,0:T(8,128)(2,1)S(1)}, u32[]{:S(2)}, u32[]{:S(2)}) async-start(bf16[32,1,1,8,576]{4,3,2,1,0:T(8,128)(2,1)} %bitcast.10), calls=%async_computation | async-start | bytes 655360 | tf_op jit(solution)/shard_map/all_to_all | solution.py:74
  109.8 373.7 %reduce-scatter.2.cloned.1.call-start = ((), (), s32[]{:S(2)}) async-start(), calls=%async_computation.3 | async-start | bytes 2162688 | tf_op jit(solution)/shard_map/reduce_scatter | solution.py:138
  270.2 214.3 %copy-start.2 = (bf16[8,512,128]{2,1,0:T(8,128)(2,1)S(1)}, bf16[8,512,128]{2,1,0:T(8,128)(2,1)}, u32[]{:S(2)}) copy-start(bf16[8,512,128]{2,1,0:T(8,128)(2,1)} %param.19) | copy-start | bytes 3145732
Sparse Core Ops, SparseCore 0:
  10.4 83.8 all-reduce.2
  270.4 213.1 reduce-scatter.1
where the time goes:
time: 493 us
  blocking collectives  336 us (68%)
  waiting for transfers between devices  106 us (22%)
  between operations  15 us (3%)
  other arithmetic  10.8 us (2%)
  starting transfers between devices  10.3 us (2%)
  matrix products  9.77 us (2%)
  local copies, waits for them, and re-layouts  5.32 us (1%)
    pmax x1, blocking collectives, on_device(): row_top = lax.pmax(local_top, 'seq')  140 us
    unnamed x1, blocking collectives  138 us
    reduce_scatter x1, waiting for transfers between devices, on_device(): lax.psum_scatter(weighted, 'seq', scatter_dimension=1, tiled=True)  72.3 us
    all_gather x1, blocking collectives, on_device(): piece = lax.all_gather(queries, 'seq', axis=1, tiled=True)  55.7 us
    psum x1, waiting for transfers between devices, on_device(): summed = lax.psum(projected, 'head')  22.8 us
    all_to_all x1, waiting for transfers between devices, on_device(): lax.all_to_all(packed, 'seq', split_axis=0, concat_axis=0, tiled=True)  10.6 us
    all_to_all x1, starting transfers between devices, on_device(): lax.all_to_all(packed, 'seq', split_axis=0, concat_axis=0, tiled=True)  10.2 us
  transfers between devices with their start and end apart: 3, of which 3 were waited for; matrix products, arithmetic and copies ran while one was open for 2% of the time, Pallas kernels for 0%

commit v1 on v0

v1 whole, which is shorter than its diff:
```python
import functools
import math

import jax
import jax.numpy as jnp
import numpy as np
from jax import lax
from jax.experimental import pallas as pl
from jax.experimental.pallas import tpu as pltpu
from jax.sharding import PartitionSpec as P

MESH = pl.DeviceIdType.MESH
BLOCK = 8
LANES = 128
MASKED = -1e30
LOWEST = -1e25
TINY = 1e-30
F32 = jnp.float32
BF16 = jnp.bfloat16


def contract_last(a, b):
    return lax.dot_general(a, b, (((1,), (1,)), ((), ())), preferred_element_type=F32)


def matmul(a, b):
    return jnp.dot(a, b, preferred_element_type=F32)


def iota(shape, dim):
    return lax.broadcasted_iota(jnp.int32, shape, dim)


def kernel(
    n_seq,
    n_head,
    lengths,
    row_prompt,
    owner,
    states,
    w_down,
    gain,
    frequency,
    queries,
    new_kv,
    w_uk,
    w_uv,
    attended,
    cache,
    part_f32,
    part_out,
    part_in,
    keys,
    query_all,
    nope_f32,
    rope_f32,
    query_full,
    new_keys,
    cache_out,
    out_f32,
    out_send,
    out_recv,
    stat_send,
    stat_recv,
    share,
    query_send_sem,
    query_recv_sem,
    part_send_sem,
    part_recv_sem,
    key_send_sem,
    key_recv_sem,
    pass_send_sem,
    pass_recv_sem,
    cache_send_sem,
    cache_recv_sem,
    half_send_sem,
    half_recv_sem,
    out_send_sem,
    out_recv_sem,
    stat_send_sem,
    stat_recv_sem,
):
    section = lax.axis_index("section")
    me = lax.axis_index("seq")
    head = lax.axis_index("head")
    prompts = lengths.shape[0]
    tokens = states.shape[0]
    chunk = tokens // n_head
    latent = gain.shape[1]
    own_queries = queries.shape[0]
    heads = w_uk.shape[0]
    nope = w_uk.shape[1]
    rope = queries.shape[1] - nope
    width = latent + LANES
    pairs = own_queries // heads
    rows = n_seq * pairs
    scale = 1.0 / math.sqrt(nope + rope)

    def seq_peer(step):
        return lax.rem(me + step, n_seq)

    def seq_back(step):
        return lax.rem(me + n_seq - step, n_seq)

    def head_peer(step):
        return lax.rem(head + step, n_head)

    def head_back(step):
        return lax.rem(head + n_head - step, n_head)

    barrier = pltpu.get_barrier_semaphore()

    @pl.loop(1, n_seq)
    def _(step):
        pl.semaphore_signal(
            barrier, inc=1, device_id=(section, seq_peer(step), head), device_id_type=MESH
        )

    @pl.loop(1, n_head)
    def _(step):
        pl.semaphore_signal(
            barrier, inc=1, device_id=(section, me, head_peer(step)), device_id_type=MESH
        )

    pl.semaphore_signal(barrier, inc=1, device_id=(1 - section, me, head), device_id_type=MESH)

    lane = iota((own_queries, LANES), 1)
    row = iota((own_queries, LANES), 0)
    second_row = lax.rem(row // heads, 2) == 1
    prompt = jnp.where(second_row, row_prompt[2 * me + 1], row_prompt[2 * me])
    query_all[0, :, nope:] = jnp.where(lane == rope + prompt, 1.0, 0.0).astype(BF16)
    query_all[0, :, : nope + rope] = queries[...]

    part = matmul(states[...], w_down[...])
    part_f32[:, : latent + rope] = part
    part_out[:, :, latent:] = jnp.zeros((n_head, chunk, LANES), BF16)
    part_out[:, :, : latent + rope] = part.astype(BF16).reshape(n_head, chunk, latent + rope)

    pl.semaphore_wait(barrier, n_seq + n_head - 1)

    @pl.loop(1, n_head)
    def _(step):
        peer = head_peer(step)
        pltpu.make_async_remote_copy(
            src_ref=part_out.at[peer],
            dst_ref=part_in.at[step - 1],
            send_sem=part_send_sem,
            recv_sem=part_recv_sem,
            device_id=(section, me, peer),
            device_id_type=MESH,
        ).start()

    @pl.loop(1, n_seq)
    def _(step):
        pltpu.make_async_remote_copy(
            src_ref=query_all.at[0],
            dst_ref=query_all.at[step],
            send_sem=query_send_sem,
            recv_sem=query_recv_sem,
            device_id=(section, seq_peer(step), head),
            device_id_type=MESH,
        ).start()

    token = (section * n_seq + me) * tokens + head * chunk + iota((chunk, LANES), 0)
    key_lane = iota((chunk, LANES), 1)
    begin = jnp.zeros((chunk, LANES), jnp.int32)
    lane_begin = jnp.zeros((chunk, LANES), jnp.int32)
    lane_end = jnp.full((chunk, LANES), 2**30, jnp.int32)
    start = jnp.int32(0)
    for p in range(prompts):
        end = start + lengths[p]
        begin = jnp.where(token >= end, end, begin)
        lane_begin = jnp.where(key_lane == rope + p, start, lane_begin)
        lane_end = jnp.where(key_lane == rope + p, end, lane_end)
        start = end
    prompt_columns = jnp.where((token >= lane_begin) & (token < lane_end), 0.0, MASKED)
    angle = (token - begin).astype(F32) * frequency[...]
    cosine = jnp.cos(angle)
    sine = jnp.sin(angle)
    signed_sine = jnp.where(key_lane < rope // 2, -sine, sine)

    new_keys[...] = jnp.zeros(new_keys.shape, BF16)
    new_keys[: new_kv.shape[0], : latent + rope] = new_kv[...]
    own_nope = queries[:, :nope].astype(F32)
    own_head = lax.rem(iota((own_queries, nope), 0), heads)
    spread = jnp.concatenate(
        [jnp.where(own_head == h, own_nope, 0.0).astype(BF16) for h in range(heads)], axis=1
    )
    own_absorbed = matmul(spread, w_uk[...].reshape(heads * nope, latent)).astype(BF16)
    own_full = jnp.concatenate([own_absorbed, query_all[0, :, nope:]], axis=1)
    own_scores = contract_last(own_full, new_keys[...]) * scale
    column = iota(own_scores.shape, 1)
    own_row = iota(own_scores.shape, 0)
    own_allowed = (
        (column < new_kv.shape[0])
        & (lax.rem(column, 2) == lax.rem(own_row // heads, 2))
        & (column // 2 <= own_row // (2 * heads))
    )
    own_scores = jnp.where(own_allowed, own_scores, MASKED)
    own_top = jnp.max(own_scores, axis=1, keepdims=True)
    own_weights = jnp.exp(own_scores - own_top)
    own_sum = jnp.sum(own_weights, axis=1, keepdims=True)
    own_context = matmul(own_weights.astype(BF16), new_keys[:, :latent]) / own_sum
    own_context = own_context.astype(BF16)
    out_head = lax.rem(iota((own_queries, LANES), 0), heads)
    own_out = jnp.zeros((own_queries, LANES), F32)
    for h in range(heads):
        own_out = jnp.where(out_head == h, matmul(own_context, w_uv[h]), own_out)

    pltpu.make_async_copy(part_in, part_in, part_recv_sem).wait()
    total = part_f32[pl.ds(pl.multiple_of(head * chunk, chunk), chunk), :]
    for k in range(n_head - 1):
        total = total + part_in[k].astype(F32)
    low = total[:, :latent]
    inverse = lax.rsqrt(jnp.mean(low * low, axis=1, keepdims=True) + 1e-06)
    keys[section, head, :, :latent] = (low * inverse * gain[...]).astype(BF16)
    tail = total[:, latent:]
    half = rope // 2
    swapped = jnp.where(
        key_lane < half, pltpu.roll(tail, LANES - half, 1), pltpu.roll(tail, half, 1)
    )
    turned = tail * cosine + swapped * signed_sine
    keys[section, head, :, latent:] = jnp.where(key_lane < rope, turned, prompt_columns).astype(
        BF16
    )

    @pl.loop(1, n_head)
    def _(step):
        pltpu.make_async_remote_copy(
            src_ref=keys.at[section, head],
            dst_ref=keys.at[section, head],
            send_sem=key_send_sem,
            recv_sem=key_recv_sem.at[step],
            device_id=(section, me, head_peer(step)),
            device_id_type=MESH,
        ).start()

    def pass_on(step):
        source = head_back(step)
        return pltpu.make_async_remote_copy(
            src_ref=keys.at[section, source],
            dst_ref=keys.at[section, source],
            send_sem=pass_send_sem,
            recv_sem=pass_recv_sem.at[step],
            device_id=(1 - section, me, head),
            device_id_type=MESH,
        )

    pass_on(0).start()

    pltpu.make_async_copy(
        query_all.at[pl.ds(1, n_seq - 1)], query_all.at[pl.ds(1, n_seq - 1)], query_recv_sem
    ).wait()
    for part_ref, lanes in ((nope_f32, slice(0, nope)), (rope_f32, slice(nope, None))):
        part_ref[...] = query_all[:, :, lanes].astype(F32).reshape(part_ref.shape)
    for h in range(heads):
        query = nope_f32[pl.ds(h, rows, stride=heads), :].astype(BF16)
        query_full[h, :, :latent] = matmul(query, w_uk[h]).astype(BF16)
        query_full[h, :, latent:] = rope_f32[pl.ds(h, rows, stride=heads), :].astype(BF16)

    for step in range(1, n_head):
        source = head_back(step)
        pltpu.make_async_copy(
            keys.at[section, source], keys.at[section, source], key_recv_sem.at[step]
        ).wait()
        pass_on(step).start()
    for step in range(n_head):
        source = head_back(step)
        pltpu.make_async_copy(
            keys.at[1 - section, source], keys.at[1 - section, source], pass_recv_sem.at[step]
        ).wait()

    all_keys = keys[...].reshape(2 * tokens, width)
    picks = []
    for s in range(2):
        owners = owner[pl.ds(s * n_seq + me, 1), :].astype(F32)
        owners = jnp.broadcast_to(owners, (16, owners.shape[1])).astype(BF16)
        expand = (
            iota((owners.shape[1], tokens), 1) // BLOCK == iota((owners.shape[1], tokens), 0)
        )
        owners = matmul(owners, jnp.where(expand, 1.0, 0.0).astype(BF16))[:1]
        slot = iota((2 * tokens, tokens), 0)
        wanted = (slot // (2 * BLOCK)).astype(F32)
        same_place = lax.rem(slot, 2 * BLOCK) == s * BLOCK + lax.rem(
            iota((2 * tokens, tokens), 1), BLOCK
        )
        picks.append(jnp.where((owners == wanted) & same_place, 1.0, 0.0).astype(BF16))
    ordered = matmul(jnp.concatenate(picks, axis=1), all_keys)
    cache_out[...] = ordered[:, : latent + rope].astype(BF16).reshape(cache_out.shape)

    half_seq = n_seq // 2
    two = 2 * BLOCK
    my_half = lax.rem(section + me // half_seq, 2)
    my_rows = pl.ds(pl.multiple_of(me * two, two), two)

    @pl.loop(0, half_seq)
    def _(step):
        peer = my_half * half_seq + lax.rem(me + step, half_seq)

        @pl.when(peer != me)
        def _():
            pltpu.make_async_remote_copy(
                src_ref=cache_out.at[peer],
                dst_ref=cache.at[my_rows],
                send_sem=cache_send_sem,
                recv_sem=cache_recv_sem,
                device_id=(section, peer, head),
                device_id_type=MESH,
            ).start()

        @pl.when(peer == me)
        def _():
            pltpu.make_async_copy(cache_out.at[me], cache.at[my_rows], cache_recv_sem).start()

    stat_lane = iota((rows, LANES), 1)
    stats = jnp.zeros((rows, LANES), F32)
    for h in range(heads):
        scores = contract_last(query_full[h], all_keys) * scale
        top = jnp.maximum(jnp.max(scores, axis=1, keepdims=True), LOWEST)
        weights = jnp.exp(scores - top)
        weight_sum = jnp.maximum(jnp.sum(weights, axis=1, keepdims=True), TINY)
        context = matmul(weights.astype(BF16), all_keys[:, :latent])
        out = matmul(context.astype(BF16), w_uv[h]) / weight_sum
        out_f32[pl.ds(h, rows, stride=heads), :] = out
        stats = jnp.where(stat_lane == h, top, stats)
        stats = jnp.where(stat_lane == heads + h, weight_sum, stats)
    stat_send[...] = stats.reshape(stat_send.shape)
    out_send[...] = out_f32[...].astype(BF16).reshape(out_send.shape)

    @pl.loop(1, n_seq)
    def _(step):
        target = (section, seq_back(step), head)
        pltpu.make_async_remote_copy(
            src_ref=stat_send.at[step],
            dst_ref=stat_recv.at[step],
            send_sem=stat_send_sem,
            recv_sem=stat_recv_sem,
            device_id=target,
            device_id_type=MESH,
        ).start()
        pltpu.make_async_remote_copy(
            src_ref=out_send.at[step],
            dst_ref=out_recv.at[step],
            send_sem=out_send_sem,
            recv_sem=out_recv_sem,
            device_id=target,
            device_id_type=MESH,
        ).start()

    stat_recv[0] = stat_send[0]
    out_recv[0] = out_send[0]

    half_rows = half_seq * two
    half_ref = cache.at[pl.ds(pl.multiple_of(my_half * half_rows, half_rows), half_rows)]
    pltpu.make_async_copy(half_ref, half_ref, cache_recv_sem).wait()
    pass_half = pltpu.make_async_remote_copy(
        src_ref=half_ref,
        dst_ref=half_ref,
        send_sem=half_send_sem,
        recv_sem=half_recv_sem,
        device_id=(1 - section, me, head),
        device_id_type=MESH,
    )
    pass_half.start()

    others = pl.ds(1, n_seq - 1)
    pltpu.make_async_copy(stat_recv.at[others], stat_recv.at[others], stat_recv_sem).wait()
    diagonal = iota((pairs, heads, LANES), 1) == iota((pairs, heads, LANES), 2)

    def compact(column):
        return jnp.sum(jnp.where(diagonal, column.reshape(pairs, heads, 1), 0.0), axis=1)

    compact_top = compact(own_top)
    compact_sum = compact(own_sum)
    tops = stat_recv[...]
    sums = pltpu.roll(tops.reshape(n_seq * pairs, LANES), LANES - heads, 1).reshape(tops.shape)
    best = jnp.maximum(jnp.max(tops, axis=0), compact_top)
    shares = jnp.exp(tops - best) * sums
    own_share = jnp.exp(compact_top - best) * compact_sum
    norm = 1.0 / (jnp.sum(shares, axis=0) + own_share)
    share[...] = shares * norm

    def expand(compacted):
        picked = jnp.where(diagonal, compacted.reshape(pairs, 1, LANES), 0.0)
        return jnp.sum(picked, axis=2, keepdims=True)

    result = expand(own_share * norm) * own_out.reshape(pairs, heads, LANES)
    pltpu.make_async_copy(out_recv.at[others], out_recv.at[others], out_recv_sem).wait()
    for step in range(n_seq):
        piece = out_recv[step].astype(F32).reshape(pairs, heads, LANES)
        result = result + expand(share[step]) * piece
    attended[...] = result.reshape(own_queries, LANES).astype(BF16)

    pltpu.make_async_copy(part_in, part_in, part_send_sem).wait()
    pltpu.make_async_copy(query_all.at[others], query_all.at[others], query_send_sem).wait()
    others_head = keys.at[section, pl.ds(0, n_head - 1)]
    pltpu.make_async_copy(others_head, others_head, key_send_sem).wait()
    pltpu.make_async_copy(keys.at[section], keys.at[section], pass_send_sem).wait()
    pltpu.make_async_copy(stat_recv.at[others], stat_recv.at[others], stat_send_sem).wait()
    pltpu.make_async_copy(out_recv.at[others], out_recv.at[others], out_send_sem).wait()
    sent = cache_out.at[pl.ds(0, half_seq - 1)]
    pltpu.make_async_copy(sent, sent, cache_send_sem).wait()

    @pl.when(my_half != me // half_seq)
    def _():
        pltpu.make_async_copy(cache_out.at[0], cache_out.at[0], cache_send_sem).wait()

    pass_half.wait_send()
    other = cache.at[pl.ds(pl.multiple_of((1 - my_half) * half_rows, half_rows), half_rows)]
    pltpu.make_async_copy(other, other, half_recv_sem).wait()


def solution(mesh):
    n_seq = mesh.shape["seq"]
    n_head = mesh.shape["head"]

    def on_device(
        prompt_states,
        w_down,
        kv_gain,
        prompt_lengths,
        block_owner,
        row_prompt,
        queries,
        new_kv,
        w_uk,
        w_uv,
    ):
        tokens = prompt_states.shape[0]
        steps, own_rows, heads, query_width = queries.shape
        latent = kv_gain.shape[0]
        total = w_down.shape[1]
        rope = total - latent
        pairs = steps * own_rows
        own_queries = pairs * heads
        width = latent + LANES
        chunk = tokens // n_head
        value = w_uv.shape[2]
        exponent = np.arange(rope // 2, dtype=np.float64)
        frequency = np.zeros((1, LANES), np.float32)
        frequency[0, :rope] = np.tile(10000.0 ** (-2.0 * exponent / rope), 2)
        vmem = pl.BlockSpec(memory_space=pltpu.VMEM)
        smem = pl.BlockSpec(memory_space=pltpu.SMEM)
        dma = pltpu.SemaphoreType.DMA
        attended, cache = pl.pallas_call(
            functools.partial(kernel, n_seq, n_head),
            out_shape=(
                jax.ShapeDtypeStruct((own_queries, value), BF16),
                jax.ShapeDtypeStruct((2 * tokens, total), BF16),
            ),
            in_specs=[smem, smem] + [vmem] * 9,
            out_specs=(vmem, pl.BlockSpec(memory_space=pl.ANY)),
            scratch_shapes=[
                pltpu.VMEM((tokens, width), F32),
                pltpu.VMEM((n_head, chunk, width), BF16),
                pltpu.VMEM((n_head - 1, chunk, width), BF16),
                pltpu.VMEM((2, n_head, chunk, width), BF16),
                pltpu.VMEM((n_seq, own_queries, 2 * LANES), BF16),
                pltpu.VMEM((n_seq * own_queries, LANES), F32),
                pltpu.VMEM((n_seq * own_queries, LANES), F32),
                pltpu.VMEM((heads, n_seq * pairs, width), BF16),
                pltpu.VMEM((LANES, width), BF16),
                pltpu.VMEM((n_seq, 2 * BLOCK, total), BF16),
                pltpu.VMEM((n_seq * own_queries, value), F32),
                pltpu.VMEM((n_seq, own_queries, value), BF16),
                pltpu.VMEM((n_seq, own_queries, value), BF16),
                pltpu.VMEM((n_seq, pairs, LANES), F32),
                pltpu.VMEM((n_seq, pairs, LANES), F32),
                pltpu.VMEM((n_seq, pairs, LANES), F32),
                dma,
                dma,
                dma,
                dma,
                dma,
                dma((n_head,)),
                dma,
                dma((n_head,)),
                dma,
                dma,
                dma,
                dma,
                dma,
                dma,
                dma,
                dma,
            ],
            compiler_params=pltpu.CompilerParams(
                collective_id=0, has_side_effects=True, vmem_limit_bytes=48 * 2**20
            ),
        )(
            prompt_lengths,
            row_prompt,
            block_owner.reshape(2 * n_seq, -1),
            prompt_states,
            w_down,
            kv_gain.reshape(1, latent),
            jnp.asarray(frequency),
            queries.reshape(own_queries, query_width),
            new_kv.reshape(pairs, total),
            w_uk,
            w_uv,
        )
        return (attended.reshape(steps, own_rows, heads, value), cache)

    placed = (
        P(("section", "seq"), "head"),
        P("head", None),
        P(),
        P(),
        P(),
        P(),
        P(None, "seq", ("section", "head"), None),
        P(None, "seq", None),
        P(("section", "head"), None, None),
        P(("section", "head"), None, None),
    )
    return jax.shard_map(
        on_device,
        mesh=mesh,
        in_specs=placed,
        out_specs=(P(None, "seq", ("section", "head"), None), P("seq", None)),
        check_vma=False,
    )
```

time: 493 us -> 64 us (0.13)
  the two profiles are of different devices: /device:TPU:8 before, /device:TPU:65 now
where the time goes in v1:
time: 64 us; the launch traced here: 63.7 us
  Pallas kernels  54.7 us (85%)
  local copies, waits for them, and re-layouts  8.24 us (13%)
  between operations  0.78 us (1%)
    pallas_call x1, Pallas kernels, on_device(): pl.pallas_call(functools.partial(kernel, n_seq, n_head), out_shape=(jax.S...  54.7 us
    unnamed x21, local copies, waits for them, and re-layouts  6.62 us

profile of v1, /device:TPU:65, one launch (start us, length us, event | category | flops | bytes accessed | tf_op | source)
XLA Modules:
  0.0 63.7 jit_solution(14628582164330500722)
XLA Ops:
  0.6 0.0 copy-start.8
  0.6 0.0 copy-start.1
  0.7 0.0 copy-start
  0.7 0.0 copy-start.4
  0.7 0.0 copy-start.7
  0.7 0.0 copy-start.6
  0.7 0.0 copy-start.5
  0.7 0.8 %reshape.22.new_kv = bf16[4,576]{1,0:T(4,128)(2,1)S(1)} reshape(bf16[2,2,576]{2,1,0:T(2,128)(2,1)} %param.18) | data formatting | bytes 9216 | tf_op jit(solution)/shard_map/reshape | solution.py:499
  1.6 0.8 %reshape.19.owner = s32[64,32]{1,0:T(8,128)S(1)} reshape(s32[2048]{0:T(1024)} %param.15) | data formatting | bytes 16384 | tf_op jit(solution)/shard_map/reshape | solution.py:493
  2.3 2.0 %copy.15.w_down = bf16[896,576]{1,0:T(8,128)(2,1)S(1)} copy(bf16[896,576]{0,1:T(8,128)(2,1)} %param.12) | data formatting | bytes 2064384 | tf_op args[1]
  4.4 0.0 copy-done.8
  4.4 0.0 copy-done.1
  4.4 0.0 copy-done
  4.4 0.0 copy-done.4
  4.4 0.0 copy-done.7
  4.4 0.0 copy-done.6
  4.4 0.0 copy-done.5
  4.4 0.0 copy-start.3
  4.4 1.0 %copy-done.3 = bf16[256,896]{1,0:T(8,128)(2,1)S(1)} copy-done((bf16[256,896]{1,0:T(8,128)(2,1)S(1)}, bf16[256,896]{1,0:T(8,128)(2,1)}, u32[]{:S(2)}) %copy-start.3) | copy-done | bytes 458776
  5.4 54.7 %shard_map.122 = (bf16[32,128]{1,0:T(8,128)(2,1)S(1)}, bf16[512,576]{1,0:T(8,128)(2,1)S(1)}) custom-call(s32[8]{0:T(128)S(1)} %copy-done.6, s32[64]{0:T(128)S(1)} %copy-done.7, s32[64,32]{1,0:T(8,128)S(1)} %reshape.19.owner, bf16[256,896]{1,0:T(8,128)(2,1)S(1)} %copy-done.3, bf16[896,576]{1,0:T(8,128)(2,1)S(1)} %copy.15.w_down, f32[1,512]{1,0:T(1,128)S(1)} %bitcast.5, ...), custom_call_target="tpu_custom_call" | custom-call | tf_op jit(solution)/shard_map/pallas_call | solution.py:445
  60.2 0.0 copy-start.2
  60.2 0.8 %copy-done.2 = bf16[512,576]{1,0:T(8,128)(2,1)} copy-done((bf16[512,576]{1,0:T(8,128)(2,1)}, bf16[512,576]{1,0:T(8,128)(2,1)S(1)}, u32[]{:S(2)}) %copy-start.2) | copy-done | bytes 589848
  61.0 2.1 %copy.16 = bf16[512,576]{0,1:T(8,128)(2,1)} copy(bf16[512,576]{1,0:T(8,128)(2,1)} %copy-done.2) | data formatting | bytes 1179648
  63.1 0.6 copy.18
Async XLA Ops:
  0.6 3.7 %copy-start.8 = (f32[1,128]{1,0:T(1,128)S(1)}, f32[1,128]{1,0:T(1,128)}, u32[]{:S(2)}) copy-start(f32[1,128]{1,0:T(1,128)} %constant.2.clone.frequency) | copy-start | bytes 1540
  0.6 3.7 %copy-start.1 = (bf16[8,512,128]{2,1,0:T(8,128)(2,1)S(1)}, bf16[8,512,128]{2,1,0:T(8,128)(2,1)}, u32[]{:S(2)}) copy-start(bf16[8,512,128]{2,1,0:T(8,128)(2,1)} %w_uv.1) | copy-start | bytes 3145732
  0.7 3.7 %copy-start = (bf16[8,128,512]{2,1,0:T(8,128)(2,1)S(1)}, bf16[8,128,512]{2,1,0:T(8,128)(2,1)}, u32[]{:S(2)}) copy-start(bf16[8,128,512]{2,1,0:T(8,128)(2,1)} %w_uk.1) | copy-start | bytes 3145732
  0.7 3.7 %copy-start.4 = (bf16[2,2,8,192]{3,2,1,0:T(8,128)(2,1)S(1)}, bf16[2,2,8,192]{3,2,1,0:T(8,128)(2,1)}, u32[]{:S(2)}) copy-start(bf16[2,2,8,192]{3,2,1,0:T(8,128)(2,1)} %param.17) | copy-start | bytes 36868
  0.7 3.7 %copy-start.7 = (s32[64]{0:T(128)S(1)}, s32[64]{0:T(128)}, u32[]{:S(2)}) copy-start(s32[64]{0:T(128)} %row_prompt.1) | copy-start | bytes 772
  0.7 3.7 %copy-start.6 = (s32[8]{0:T(128)S(1)}, s32[8]{0:T(128)}, u32[]{:S(2)}) copy-start(s32[8]{0:T(128)} %lengths.1) | copy-start | bytes 100
  0.7 3.7 %copy-start.5 = (f32[512]{0:T(512)S(1)}, f32[512]{0:T(512)}, u32[]{:S(2)}) copy-start(f32[512]{0:T(512)} %param.13) | copy-start | bytes 6148
  4.4 1.0 %copy-start.3 = (bf16[256,896]{1,0:T(8,128)(2,1)S(1)}, bf16[256,896]{1,0:T(8,128)(2,1)}, u32[]{:S(2)}) copy-start(bf16[256,896]{1,0:T(8,128)(2,1)} %states.1) | copy-start | bytes 1376260
  60.2 0.8 %copy-start.2 = (bf16[512,576]{1,0:T(8,128)(2,1)}, bf16[512,576]{1,0:T(8,128)(2,1)S(1)}, u32[]{:S(2)}) copy-start(bf16[512,576]{1,0:T(8,128)(2,1)S(1)} %get-tuple-element.9) | copy-start | bytes 1769476
